TPU v7x, 32 devices: a whole 2x2x4 slice. The times are simulated.
32 devices in a mesh: section: 2 (over core), dp: 16 (over z, y, x).
Axes of the slice: x: 2, y: 2, z: 4, core: 2. Of those that a mesh axis runs over, the one named last changes fastest.
Arguments:
- tokens: bfloat16 [2, 10240, 768], P(None, 'dp'), may hold values from -6 to 6
- segment_ids: int32 [2, 10240], P(None, 'dp'), may hold values from 0 to 7, as said below
- keep_masks: int32 [2, 2, 2, 128], P('section', None, None, 'dp'), may hold values 0 or 1
- cotangent: bfloat16 [2, 10240, 768], P(None, 'dp'), may hold values from -6 to 6
- norm1_gain: float32 [2, 768], P('section'), may hold values from 0.5 to 1.5
- norm1_bias: float32 [2, 768], P('section'), may hold values from -1.25 to 1.25
- qkv_weight: bfloat16 [2, 768, 2304], P('section'), may hold values from -0.21875 to 0.21875
- qv_bias: float32 [2, 1536], P('section'), may hold values from -1.25 to 1.25
- out_weight: bfloat16 [2, 768, 768], P('section'), may hold values from -0.875 to 0.875
- out_bias: float32 [2, 768], P('section'), may hold values from -1.25 to 1.25
- norm2_gain: float32 [2, 768], P('section'), may hold values from 0.5 to 1.5
- norm2_bias: float32 [2, 768], P('section'), may hold values from -1.25 to 1.25
- fc1_weight: bfloat16 [2, 768, 3072], P('section'), may hold values from -0.21875 to 0.21875
- fc1_bias: float32 [2, 3072], P('section'), may hold values from -1.25 to 1.25
- fc2_weight: bfloat16 [2, 3072, 768], P('section'), may hold values from -0.109375 to 0.109375
- fc2_bias: float32 [2, 768], P('section'), may hold values from -1.25 to 1.25
Outputs:
- layer_out: bfloat16 [2, 2, 10240, 768], P('section', None, 'dp')
- input_grad: bfloat16 [2, 2, 10240, 768], P('section', None, 'dp')
- grad_norm1_gain: float32 [2, 768], P('section', 'dp')
- grad_norm1_bias: float32 [2, 768], P('section', 'dp')
- grad_qkv_weight: float32 [2, 768, 2304], P('section', 'dp')
- grad_qv_bias: float32 [2, 1536], P('section', 'dp')
- grad_out_weight: float32 [2, 768, 768], P('section', 'dp')
- grad_out_bias: float32 [2, 768], P('section', 'dp')
- grad_norm2_gain: float32 [2, 768], P('section', 'dp')
- grad_norm2_bias: float32 [2, 768], P('section', 'dp')
- grad_fc1_weight: float32 [2, 768, 3072], P('section', 'dp')
- grad_fc1_bias: float32 [2, 3072], P('section', 'dp')
- grad_fc2_weight: float32 [2, 3072, 768], P('section', 'dp')
- grad_fc2_bias: float32 [2, 768], P('section', 'dp')
Inputs may be any that keep to these rules, and one draw needn't show every extreme that they name: `segment_ids`: within each aligned block of 640 slots the ids never fall; from the block's start it holds one image of 578 tokens, or three of 198, or six of 102, or two of 198 then two of 102, or one of 198 then four of 102, numbered from 0; the remaining slots of the block carry id 7.
All inputs are finite; a program needn't handle non-finite values. No bound on the sum of `keep_masks` on one device may be relied on, other than what follows from the above.
Results may differ from a plain program's by a relative error of at most 0.014.
Values may be sent and summed in bfloat16 or wider, within the bound.
A program may use at most 384 MiB of HBM per device.

v0:
```python
import jax
import jax.numpy as jnp
from jax import lax
from jax.sharding import PartitionSpec as P

HEAD_DIM = 64


keep_rate = 0.9
norm_eps = 1e-06
root_half = 0.7071067811865476
inverse_root = 0.3989422804014327


def passed_along(block, axis, distance):
    devices = range(lax.axis_size(axis))
    route = [(i - distance, i) for i in devices if i - distance in devices]
    return lax.ppermute(block, axis, route)


def normalize(values, gain, shift):
    center = values - jnp.mean(values, axis=-1, keepdims=True)
    scale = lax.rsqrt(jnp.mean(center * center, axis=-1, keepdims=True) + norm_eps)
    unit = center * scale
    return (unit * gain + shift, unit, scale)


def normalize_back(grad, unit, scale, gain):
    scaled = grad * gain
    inner = jnp.mean(scaled, axis=-1, keepdims=True)
    along = jnp.mean(scaled * unit, axis=-1, keepdims=True)
    return scale * (scaled - inner - unit * along)


def attention_scores(queries, keys, segment):
    scores = jnp.einsum(
        "qhd,khd->hqk", queries, keys, preferred_element_type=jnp.float32
    ) * HEAD_DIM ** (-0.5)
    same = segment[:, None] == segment[None, :]
    return jnp.where(same[None], scores, -1000000000.0)


def forward_layer(inputs, keep_tok, segment, params):
    (
        gain_one,
        shift_one,
        w_qkv,
        bias_qv,
        w_out,
        bias_out,
        gain_two,
        shift_two,
        w_up,
        bias_up,
        w_down,
        bias_down,
    ) = params
    width = inputs.shape[1]
    heads = width // HEAD_DIM
    normed, unit_one, scale_one = normalize(inputs, gain_one, shift_one)
    normed_low = normed.astype(jnp.bfloat16)
    mixed = jnp.dot(normed_low, w_qkv, preferred_element_type=jnp.float32)
    queries = (mixed[:, :width] + bias_qv[:width]).astype(jnp.bfloat16).reshape(-1, heads, HEAD_DIM)
    keys = mixed[:, width : 2 * width].astype(jnp.bfloat16).reshape(-1, heads, HEAD_DIM)
    values = (
        (mixed[:, 2 * width :] + bias_qv[width:]).astype(jnp.bfloat16).reshape(-1, heads, HEAD_DIM)
    )
    scores = attention_scores(queries, keys, segment)
    peak = jnp.max(scores, axis=-1, keepdims=True)
    raised = jnp.exp(scores - peak)
    total = jnp.sum(raised, axis=-1, keepdims=True)
    weights = (raised / total).astype(jnp.bfloat16)
    logsum = peak + jnp.log(total)
    attended = jnp.einsum("hqk,khd->qhd", weights, values, preferred_element_type=jnp.float32)
    attended = attended.reshape(-1, width).astype(jnp.bfloat16)
    branch = jnp.dot(attended, w_out, preferred_element_type=jnp.float32) + bias_out
    middle = inputs + keep_tok[:, 0:1] * branch / keep_rate
    second, unit_two, scale_two = normalize(middle, gain_two, shift_two)
    second_low = second.astype(jnp.bfloat16)
    hidden = jnp.dot(second_low, w_up, preferred_element_type=jnp.float32) + bias_up
    active_low = jax.nn.gelu(hidden, approximate=False).astype(jnp.bfloat16)
    branch_two = jnp.dot(active_low, w_down, preferred_element_type=jnp.float32) + bias_down
    output = middle + keep_tok[:, 1:2] * branch_two / keep_rate
    saved = (
        unit_one,
        scale_one,
        normed_low,
        queries,
        keys,
        values,
        logsum,
        attended,
        unit_two,
        scale_two,
        second_low,
        hidden,
        active_low,
    )
    return (output, saved)


def backward_layer(upstream, keep_tok, segment, params, saved):
    (
        gain_one,
        shift_one,
        w_qkv,
        bias_qv,
        w_out,
        bias_out,
        gain_two,
        shift_two,
        w_up,
        bias_up,
        w_down,
        bias_down,
    ) = params
    (
        unit_one,
        scale_one,
        normed_low,
        queries,
        keys,
        values,
        logsum,
        attended,
        unit_two,
        scale_two,
        second_low,
        hidden,
        active_low,
    ) = saved
    width = upstream.shape[1]
    heads = width // HEAD_DIM
    grad_down = (keep_tok[:, 1:2] * upstream / keep_rate).astype(jnp.bfloat16)
    grad_active = jnp.einsum("td,fd->tf", grad_down, w_down, preferred_element_type=jnp.float32)
    slope = (
        0.5 * (1.0 + lax.erf(hidden * root_half))
        + hidden * jnp.exp(-0.5 * hidden * hidden) * inverse_root
    )
    grad_hidden = (grad_active * slope).astype(jnp.bfloat16)
    grad_second = jnp.einsum("tf,df->td", grad_hidden, w_up, preferred_element_type=jnp.float32)
    grad_middle = upstream + normalize_back(grad_second, unit_two, scale_two, gain_two)
    grad_branch = (keep_tok[:, 0:1] * grad_middle / keep_rate).astype(jnp.bfloat16)
    grad_attended = jnp.einsum("td,ed->te", grad_branch, w_out, preferred_element_type=jnp.float32)
    grad_attended = grad_attended.astype(jnp.bfloat16).reshape(-1, heads, HEAD_DIM)
    scores = attention_scores(queries, keys, segment)
    probs = jnp.exp(scores - logsum)
    weights = probs.astype(jnp.bfloat16)
    grad_weights = jnp.einsum(
        "qhd,khd->hqk", grad_attended, values, preferred_element_type=jnp.float32
    )
    grad_values = jnp.einsum(
        "hqk,qhd->khd", weights, grad_attended, preferred_element_type=jnp.float32
    )
    grad_scores = probs * (grad_weights - jnp.sum(grad_weights * probs, axis=-1, keepdims=True))
    grad_scores = grad_scores.astype(jnp.bfloat16)
    grad_queries = jnp.einsum(
        "hqk,khd->qhd", grad_scores, keys, preferred_element_type=jnp.float32
    ) * HEAD_DIM ** (-0.5)
    grad_keys = jnp.einsum(
        "hqk,qhd->khd", grad_scores, queries, preferred_element_type=jnp.float32
    ) * HEAD_DIM ** (-0.5)
    grad_mixed = jnp.concatenate(
        [
            grad_queries.reshape(-1, width),
            grad_keys.reshape(-1, width),
            grad_values.reshape(-1, width),
        ],
        axis=1,
    ).astype(jnp.bfloat16)
    grad_normed = jnp.einsum("tc,dc->td", grad_mixed, w_qkv, preferred_element_type=jnp.float32)
    grad_input = grad_middle + normalize_back(grad_normed, unit_one, scale_one, gain_one)
    operands = (
        unit_one,
        grad_normed,
        normed_low,
        grad_mixed,
        attended,
        grad_branch,
        unit_two,
        grad_second,
        second_low,
        grad_hidden,
        active_low,
        grad_down,
    )
    return (grad_input, operands)


def weight_grads(operands):
    (
        unit_one,
        grad_normed,
        normed_low,
        grad_mixed,
        attended,
        grad_branch,
        unit_two,
        grad_second,
        second_low,
        grad_hidden,
        active_low,
        grad_down,
    ) = operands
    width = unit_one.shape[1]
    mixed_sum = jnp.sum(grad_mixed, axis=0, dtype=jnp.float32)
    return (
        jnp.sum(grad_normed * unit_one, axis=0),
        jnp.sum(grad_normed, axis=0),
        jnp.einsum("td,tc->dc", normed_low, grad_mixed, preferred_element_type=jnp.float32),
        jnp.concatenate([mixed_sum[:width], mixed_sum[2 * width :]]),
        jnp.einsum("td,te->de", attended, grad_branch, preferred_element_type=jnp.float32),
        jnp.sum(grad_branch, axis=0, dtype=jnp.float32),
        jnp.sum(grad_second * unit_two, axis=0),
        jnp.sum(grad_second, axis=0),
        jnp.einsum("td,tf->df", second_low, grad_hidden, preferred_element_type=jnp.float32),
        jnp.sum(grad_hidden, axis=0, dtype=jnp.float32),
        jnp.einsum("tf,td->fd", active_low, grad_down, preferred_element_type=jnp.float32),
        jnp.sum(grad_down, axis=0, dtype=jnp.float32),
    )


def blank_forward(rows, width, inner, heads):
    return (
        jnp.zeros((rows, width), jnp.float32),
        (
            jnp.zeros((rows, width), jnp.float32),
            jnp.zeros((rows, 1), jnp.float32),
            jnp.zeros((rows, width), jnp.bfloat16),
            jnp.zeros((rows, heads, HEAD_DIM), jnp.bfloat16),
            jnp.zeros((rows, heads, HEAD_DIM), jnp.bfloat16),
            jnp.zeros((rows, heads, HEAD_DIM), jnp.bfloat16),
            jnp.zeros((heads, rows, 1), jnp.float32),
            jnp.zeros((rows, width), jnp.bfloat16),
            jnp.zeros((rows, width), jnp.float32),
            jnp.zeros((rows, 1), jnp.float32),
            jnp.zeros((rows, width), jnp.bfloat16),
            jnp.zeros((rows, inner), jnp.float32),
            jnp.zeros((rows, inner), jnp.bfloat16),
        ),
    )


def sum_once(grads):
    (
        gain_one,
        shift_one,
        w_qkv,
        bias_qv,
        w_out,
        bias_out,
        gain_two,
        shift_two,
        w_up,
        bias_up,
        w_down,
        bias_down,
    ) = grads
    return (
        lax.psum_scatter(gain_one, "dp", scatter_dimension=0, tiled=True),
        lax.psum_scatter(shift_one, "dp", scatter_dimension=0, tiled=True),
        lax.psum_scatter(w_qkv, "dp", scatter_dimension=0, tiled=True),
        lax.psum_scatter(bias_qv, "dp", scatter_dimension=0, tiled=True),
        lax.psum_scatter(w_out, "dp", scatter_dimension=0, tiled=True),
        lax.psum_scatter(bias_out, "dp", scatter_dimension=0, tiled=True),
        lax.psum_scatter(gain_two, "dp", scatter_dimension=0, tiled=True),
        lax.psum_scatter(shift_two, "dp", scatter_dimension=0, tiled=True),
        lax.psum_scatter(w_up, "dp", scatter_dimension=0, tiled=True),
        lax.psum_scatter(bias_up, "dp", scatter_dimension=0, tiled=True),
        lax.psum_scatter(w_down, "dp", scatter_dimension=0, tiled=True),
        lax.psum_scatter(bias_down, "dp", scatter_dimension=0, tiled=True),
    )


def shards(
    tokens,
    segment_ids,
    keep_masks,
    cotangent,
    norm1_gain,
    norm1_bias,
    qkv_weight,
    qv_bias,
    out_weight,
    out_bias,
    norm2_gain,
    norm2_bias,
    fc1_weight,
    fc1_bias,
    fc2_weight,
    fc2_bias,
):
    params = tuple(
        (
            weight[0]
            for weight in (
                norm1_gain,
                norm1_bias,
                qkv_weight,
                qv_bias,
                out_weight,
                out_bias,
                norm2_gain,
                norm2_bias,
                fc1_weight,
                fc1_bias,
                fc2_weight,
                fc2_bias,
            )
        )
    )
    first_section = lax.axis_index("section") == 0
    micro, rows, width = tokens.shape
    inner = fc1_weight.shape[2]
    heads = width // HEAD_DIM
    table = keep_masks[0].astype(jnp.float32)
    slots = jnp.arange(table.shape[2], dtype=jnp.int32)

    def pick(first_value, second_value):
        return jnp.where(first_section, first_value, second_value)

    def token_keep(index):
        onehot = (segment_ids[index][:, None] == slots[None, :]).astype(jnp.float32)
        return jnp.sum(onehot[:, None, :] * table[index][None, :, :], axis=2)

    received = jnp.zeros((rows, width), jnp.bfloat16)
    outputs = []
    kept = []
    for tick in range(micro + 1):
        early = min(tick, micro - 1)
        late = max(tick - 1, 0)
        live = pick(tick < micro, tick >= 1)
        inputs = pick(tokens[early], received).astype(jnp.float32)
        keep_tok = pick(token_keep(early), token_keep(late))
        segment = pick(segment_ids[early], segment_ids[late])
        result, saved = lax.cond(
            live,
            lambda: forward_layer(inputs, keep_tok, segment, params),
            lambda: blank_forward(rows, width, inner, heads),
        )
        outputs.append(result)
        kept.append(saved)
        if tick < micro:
            received = passed_along(result.astype(jnp.bfloat16), "section", 1)
    layer_out = jnp.stack(
        [pick(outputs[index], outputs[index + 1]) for index in range(micro)]
    ).astype(jnp.bfloat16)[None]
    returned = jnp.zeros((rows, width), jnp.bfloat16)
    grads_in = []
    pieces = []
    for tick in range(micro + 1):
        early = min(micro - tick, micro - 1)
        late = max(micro - 1 - tick, 0)
        live = pick(tick >= 1, tick < micro)
        upstream = pick(returned, cotangent[late]).astype(jnp.float32)
        keep_tok = pick(token_keep(early), token_keep(late))
        segment = pick(segment_ids[early], segment_ids[late])
        saved = kept[micro - tick]

        def run_back():
            grad_input, operands = backward_layer(upstream, keep_tok, segment, params, saved)
            return (grad_input, weight_grads(operands))

        def run_blank():
            return (
                jnp.zeros((rows, width), jnp.float32),
                tuple((jnp.zeros(weight.shape, jnp.float32) for weight in params)),
            )

        grad_input, piece = lax.cond(live, run_back, run_blank)
        grads_in.append(grad_input)
        pieces.append(piece)
        if tick < micro:
            returned = passed_along(grad_input.astype(jnp.bfloat16), "section", -1)
    input_grad = jnp.stack(
        [pick(grads_in[micro - index], grads_in[micro - 1 - index]) for index in range(micro)]
    ).astype(jnp.bfloat16)[None]
    chosen = [jax.tree.map(pick, pieces[index + 1], pieces[index]) for index in range(micro)]
    total = chosen[0]
    for piece in chosen[1:]:
        total = jax.tree.map(jnp.add, total, piece)
    summed = sum_once(total)
    return (
        layer_out,
        input_grad,
        summed[0][None],
        summed[1][None],
        summed[2][None],
        summed[3][None],
        summed[4][None],
        summed[5][None],
        summed[6][None],
        summed[7][None],
        summed[8][None],
        summed[9][None],
        summed[10][None],
        summed[11][None],
    )


def solution(mesh):
    in_specs = (
        P(None, "dp", None),
        P(None, "dp"),
        P("section", None, None, "dp"),
        P(None, "dp", None),
        P("section", None),
        P("section", None),
        P("section", None, None),
        P("section", None),
        P("section", None, None),
        P("section", None),
        P("section", None),
        P("section", None),
        P("section", None, None),
        P("section", None),
        P("section", None, None),
        P("section", None),
    )
    out_specs = (
        P("section", None, "dp", None),
        P("section", None, "dp", None),
        P("section", "dp"),
        P("section", "dp"),
        P("section", "dp", None),
        P("section", "dp"),
        P("section", "dp", None),
        P("section", "dp"),
        P("section", "dp"),
        P("section", "dp"),
        P("section", "dp", None),
        P("section", "dp"),
        P("section", "dp", None),
        P("section", "dp"),
    )
    return jax.shard_map(shards, mesh=mesh, in_specs=in_specs, out_specs=out_specs, check_vma=False)
```

profile of v0, /device:TPU:0, one launch (start us, length us, event | category | flops | bytes accessed | tf_op | source)
XLA Modules:
  0.0 1320.4 jit_solution(11852142032813041311)
XLA Ops:
  10.6 93.8 %conditional.4 = (f32[640,768]{1,0:T(8,128)S(1)}, f32[640,768]{1,0:T(8,128)}, f32[640,1]{0,1:T(1,128)S(1)}, bf16[640,768]{1,0:T(8,128)(2,1)}, bf16[640,12,64]{0,...) conditional(s32[]{:T(128)} %convert_element_type.288, () %tuple.46, ...), branch_computations={%region_1.2_spmd, %region_2.9_spmd} | conditional | flops 10524829696 | bytes 185566064 | solution.py:336
  17.0 3.7 fusion.156
  20.7 2.5 copy-done.27
  29.0 11.4 fusion
  40.4 10.6 fusion.1
  51.0 13.8 %fusion.20 = bf16[12,64,640]{2,1,0:T(8,128)(2,1)} fusion(bf16[640,12,64]{0,2,1:T(8,128)(2,1)} %bitcast.1, f32[12,640,640]{1,2,0:T(8,128)} %get-tuple-element.816, f32[12,640]{1,0:T(8,128)S(1)} %fusion.1, f32[12,640]{1,0:T(8,128)S(1)} %get-tuple-element.815, pred[640,640]{0,1:T(8,128)(4,1)S(1)} %broadcast_compare_fusion), kind=kOutput, calls=%fused_computation.43 | convolution fusion | flops 654213120 | bytes 22097920 | tf_op jit(solution)/shard_map/cond/branch_1_fun/hqk,khd->qhd/dot_general | solution.py:74
  64.8 3.6 fusion.148
  70.4 3.6 add_convert_fusion
  74.0 22.8 %fusion.5 = (bf16[640,3072]{1,0:T(8,128)(2,1)}, f32[640,3072]{1,0:T(8,128)}) fusion(f32[3072]{0:T(1024)S(1)} %bitcast.341, bf16[640,768]{1,0:T(8,128)(2,1)} %get-tuple-element.904, bf16[768,3072]{1,0:T(8,128)(2,1)} %get-tuple-element.233), kind=kOutput, calls=%fused_computation.9 | convolution fusion | flops 3149660160 | bytes 17510400 | tf_op jit(solution)/shard_map/cond/branch_1_fun/dot_general | solution.py:80
  96.8 7.3 multiply_add_fusion
  114.3 4.7 fusion.137
  124.2 8.5 fusion.154
  132.7 9.3 fusion.75
  142.1 8.6 fusion.115
  152.5 21.8 %fusion.83 = (bf16[640,3072]{1,0:T(8,128)(2,1)S(1)}, f32[640,3072]{1,0:T(8,128)}) fusion(f32[3072]{0:T(1024)S(1)} %bitcast.340, bf16[1,768,3072]{2,1,0:T(8,128)(2,1)S(1)} %bitcast.314, f32[640,768]{1,0:T(8,128)S(1)} %get-tuple-element.862, f32[768]{0:T(1024)S(1)} %reduce.40, f32[768]{0:T(1024)S(1)} %reduce.39, f32[640]{0:T(1024)S(1)} %add_rsqrt_fusion.4, ...), kind=kOutput, calls=%fused_computation.219 | convolution fusion | flops 3152117760 | bytes 18504704 | tf_op jit(solution)/shard_map/cond/branch_1_fun/dot_general | solution.py:80
  174.5 3.2 multiply_add_fusion.6
  182.6 22.0 %conditional.5 = (f32[640,768]{1,0:T(8,128)S(1)}, f32[640,768]{1,0:T(8,128)}, f32[640,1]{0,1:T(1,128)S(1)}, bf16[640,768]{1,0:T(8,128)(2,1)}, bf16[640,12,64]{0,...) conditional(s32[]{:T(128)} %convert_element_type.305, () %tuple.48, ...), branch_computations={%region_16.17_spmd, %region_17.24_spmd} | conditional | flops 10522372096 | bytes 199291728 | solution.py:336
  191.0 4.1 broadcast.773
  195.0 2.4 broadcast.774
  205.9 23.8 %conditional.6 = (bf16[640,768]{1,0:T(8,128)(2,1)}, f32[768]{0:T(1024)S(1)}, f32[768]{0:T(1024)S(1)}, f32[1536]{0:T(1024)S(1)}, f32[768]{0:T(1024)S(1)}, /*index...) conditional(s32[]{:T(128)} %convert_element_type.305, () %tuple.51, ...), branch_computations={%region_24.25_spmd, %region_25.39_spmd} | conditional | flops 21413953536 | bytes 418371616 | solution.py:370
  206.9 3.4 broadcast.811.clone
  211.9 4.8 broadcast.814.clone
  216.7 4.1 broadcast.816.clone
  231.1 204.5 %collective-permute-done.2 = bf16[640,768]{1,0:T(8,128)(2,1)S(1)} collective-permute-done((bf16[640,768]{1,0:T(8,128)(2,1)}, bf16[640,768]{1,0:T(8,128)(2,1)S(1)}, u32[]{:S(2)}, u32[]{:S(2)}) %collective-permute-start.2) | collective-permute-done | bytes 983072 | tf_op jit(solution)/shard_map/ppermute | solution.py:18
  435.6 2.4 convert_reduce_fusion.12
  438.0 9.4 convert_reduce_fusion.9
  447.6 4.2 multiply_reduce_fusion.18
  458.2 10.9 fusion.116
  469.1 12.4 multiply_reduce_fusion.17
  481.5 13.9 %multiply_convert_fusion.9 = bf16[12,640,640]{1,2,0:T(8,128)(2,1)S(1)} fusion(f32[12,640,640]{1,2,0:T(8,128)} %get-tuple-element.867, f32[12,640,640]{1,2,0:T(8,128)} %get-tuple-element.860, f32[12,640]{1,0:T(8,128)S(1)} %get-tuple-element.866, f32[12,640]{1,0:T(8,128)S(1)} %log_add_fusion), kind=kLoop, calls=%fused_computation.202 | loop fusion | flops 19660800 | bytes 49213440 | tf_op jit(solution)/shard_map/cond/branch_1_fun/convert_element_type | solution.py:156
  495.4 5.5 multiply_convert_fusion.10
  504.1 3.5 fusion.109
  511.2 2.5 fusion.160
  514.6 155.4 %conditional.7 = (bf16[640,768]{1,0:T(8,128)(2,1)}, f32[768]{0:T(1024)S(1)}, f32[768]{0:T(1024)S(1)}, f32[1536]{0:T(1024)S(1)}, f32[768]{0:T(1024)S(1)}, /*index...) conditional(s32[]{:T(128)} %convert_element_type.288, () %tuple.50, ...), branch_computations={%region_44.45_spmd, %region_45.59_spmd} | conditional | flops 21411987456 | bytes 420730880 | solution.py:370
  516.7 9.0 convert_reduce_fusion.5
  525.8 7.7 multiply_reduce_fusion.11
  533.5 4.5 convert_reduce_fusion.8
  538.0 2.5 convolution_convert_fusion.1
  541.4 10.7 fusion.159
  552.4 12.4 fusion.69
  564.8 13.7 %multiply_reduce_fusion.10 = (f32[12,640]{1,0:T(8,128)S(1)}, f32[12,640,640]{1,2,0:T(8,128)}) fusion(f32[12,640,640]{1,2,0:T(8,128)} %fusion.159, f32[12,640]{1,0:T(8,128)S(1)} %bitcast.303, pred[640,640]{0,1:T(8,128)(4,1)S(1)} %broadcast_compare_fusion.3, bf16[640,12,64]{0,2,1:T(8,128)(2,1)S(1)} %bitcast.286, bf16[640,12,64]{0,2,1:T(8,128)(2,1)} %get-tuple-element.288), kind=kOutput, calls=%fused_computation.156 | convolution fusion | flops 653713920 | bytes 41758720 | tf_op jit(solution)/shard_map/cond/branch_1_fun/qhd,khd->hqk/dot_general | solution.py:149
  578.5 14.2 %multiply_convert_fusion.4 = bf16[12,640,640]{1,2,0:T(8,128)(2,1)S(1)} fusion(f32[12,640,640]{1,2,0:T(8,128)} %get-tuple-element.845, f32[12,640,640]{1,2,0:T(8,128)} %fusion.159, f32[12,640]{1,0:T(8,128)S(1)} %get-tuple-element.844, f32[12,640]{1,0:T(8,128)S(1)} %bitcast.304, pred[640,640]{0,1:T(8,128)(4,1)S(1)} %broadcast_compare_fusion.3), kind=kLoop, calls=%fused_computation.155 | loop fusion | flops 29491200 | bytes 49623040 | tf_op jit(solution)/shard_map/cond/branch_1_fun/convert_element_type | solution.py:156
  592.7 5.4 multiply_convert_fusion.5
  600.7 5.6 multiply_reduce_fusion.12
  606.3 3.7 multiply_add_fusion.4
  610.6 9.0 convolution_bitcast_fusion.6
  619.5 8.1 copy.213
  632.1 9.9 convolution_bitcast_fusion.5
  642.0 9.7 copy.217
  651.7 8.4 convolution_bitcast_fusion.4
  660.1 9.7 copy.219
  670.0 4.4 select_add_fusion.3
  674.5 7.4 fusion.139
  681.9 9.4 select_add_fusion.2
  692.9 6.3 fusion.142
  699.3 7.5 select_add_fusion.1
  708.0 6.1 fusion.161
  714.1 7.3 select_add_fusion
  724.6 3.0 fusion.119
  728.3 79.0 %all-reduce.8 = (f32[768]{0:T(1024)S(1)}, f32[768]{0:T(1024)S(1)}, f32[1536]{0:T(1024)S(1)}, f32[768]{0:T(1024)S(1)}, f32[768]{0:T(1024)S(1)}, /*index=5*/f32[76...) all-reduce(f32[768]{0:T(1024)S(1)} %get-tuple-element.876, ...), channel_id=2, replica_groups=mesh['section'=2,'dp'=16] {'dp'}, use_global_device_ids=true, to_apply=%region_60.61.clone | all-reduce | flops 9216 | bytes 73728
  813.4 3.5 pad_maximum_fusion.9
  816.9 144.5 %reduce-scatter.5.cloned.1.call-done = f32[48,2304]{1,0:T(8,128)} async-done(((f32[768,2304]{1,0:T(8,128)}), f32[48,2304]{1,0:T(8,128)}) %reduce-scatter.5.cloned.1.call-update) | async-done | bytes 442384 | tf_op jit(solution)/shard_map/reduce_scatter | solution.py:262
  961.4 176.3 %reduce-scatter.9.cloned.1.call-done = f32[48,3072]{1,0:T(8,128)} async-done(((f32[768,3072]{1,0:T(8,128)}), f32[48,3072]{1,0:T(8,128)}) %reduce-scatter.9.cloned.1.call-update) | async-done | bytes 589840 | tf_op jit(solution)/shard_map/reduce_scatter | solution.py:268
  1137.7 175.9 %reduce-scatter.11.cloned.1.call-done = f32[192,768]{1,0:T(8,128)} async-done(((f32[3072,768]{1,0:T(8,128)}), f32[192,768]{1,0:T(8,128)}) %reduce-scatter.11.cloned.1.call-update) | async-done | bytes 589840 | tf_op jit(solution)/shard_map/reduce_scatter | solution.py:270
  (424 shorter events, 87.6 us)
Async XLA Ops:
  7.2 809.7 %reduce-scatter.7.cloned.1.call-start = ((), (), s32[]{:S(2)}) async-start(), calls=%async_computation.5 | async-start | bytes 2506752 | tf_op jit(solution)/shard_map/reduce_scatter | solution.py:264
  8.7 102.7 %copy-start.73 = (s32[640]{0:T(1024)}, s32[640]{0:T(1024)S(1)}, u32[]{:S(2)}) copy-start(s32[640]{0:T(1024)S(1)} %get-tuple-element.773) | copy-start | bytes 7684
  8.8 102.5 %copy-start.79 = (f32[640,2]{0,1:T(2,128)}, f32[640,2]{0,1:T(2,128)S(1)}, u32[]{:S(2)}) copy-start(f32[640,2]{0,1:T(2,128)S(1)} %multiply_reduce_fusion.24) | copy-start | bytes 15364
  9.6 101.6 %copy-start.98 = (f32[1,1536]{1,0:T(1,128)S(1)}, f32[1,1536]{1,0:T(1,128)}, u32[]{:S(2)}) copy-start(f32[1,1536]{1,0:T(1,128)} %param.31) | copy-start | bytes 18436
  29.0 11.4 copy-start
  51.0 13.8 %copy-start.140 = (bf16[768,768]{1,0:T(8,128)(2,1)S(1)}, bf16[768,768]{1,0:T(8,128)(2,1)}, u32[]{:S(2)}) copy-start(bf16[768,768]{1,0:T(8,128)(2,1)} %get-tuple-element.229) | copy-start | bytes 3538948 | tf_op jit(solution)/shard_map/cond
  74.0 22.8 %copy-start.97 = (f32[1,768]{1,0:T(1,128)S(1)}, f32[1,768]{1,0:T(1,128)}, u32[]{:S(2)}) copy-start(f32[1,768]{1,0:T(1,128)} %get-tuple-element.236) | copy-start | bytes 9220 | tf_op jit(solution)/shard_map/cond
  104.4 14.6 %copy-start.4 = (f32[640,768]{1,0:T(8,128)}, f32[640,768]{1,0:T(8,128)S(1)}, u32[]{:S(2)}) copy-start(f32[640,768]{1,0:T(8,128)S(1)} %get-tuple-element.364) | copy-start | bytes 5898244
  104.4 14.6 %copy-start.62 = (f32[12,640,1]{1,0,2:T(8,128)}, f32[12,640,1]{1,0,2:T(8,128)S(1)}, u32[]{:S(2)}) copy-start(f32[12,640,1]{1,0,2:T(8,128)S(1)} %get-tuple-element.386) | copy-start | bytes 92164
  104.4 14.6 %copy-start.122 = (f32[640,1]{0,1:T(1,128)}, f32[640,1]{0,1:T(1,128)S(1)}, u32[]{:S(2)}) copy-start(f32[640,1]{0,1:T(1,128)S(1)} %get-tuple-element.383) | copy-start | bytes 7684
  104.4 14.6 %copy-start.124 = (f32[640,1]{0,1:T(1,128)}, f32[640,1]{0,1:T(1,128)S(1)}, u32[]{:S(2)}) copy-start(f32[640,1]{0,1:T(1,128)S(1)} %get-tuple-element.366) | copy-start | bytes 7684
  105.6 6.7 collective-permute-start
  108.4 10.7 copy-start.126
  109.1 10.0 copy-start.103
  109.8 42.7 %copy-start.75 = (f32[768]{0:T(1024)}, f32[768]{0:T(1024)S(1)}, u32[]{:S(2)}) copy-start(f32[768]{0:T(1024)S(1)} %reduce.40) | copy-start | bytes 9220
  110.5 42.0 %copy-start.70 = (f32[768]{0:T(1024)}, f32[768]{0:T(1024)S(1)}, u32[]{:S(2)}) copy-start(f32[768]{0:T(1024)S(1)} %reduce.39) | copy-start | bytes 9220
  112.0 38.8 %copy-start.101 = (f32[640]{0:T(1024)}, f32[640]{0:T(1024)S(1)}, u32[]{:S(2)}) copy-start(f32[640]{0:T(1024)S(1)} %get-tuple-element.771) | copy-start | bytes 7684
  112.0 62.4 %copy-start.106 = (f32[640]{0:T(1024)}, f32[640]{0:T(1024)S(1)}, u32[]{:S(2)}) copy-start(f32[640]{0:T(1024)S(1)} %get-tuple-element.770) | copy-start | bytes 7684
  121.6 20.4 %copy-start.30 = (bf16[640,768]{0,1:T(8,128)(2,1)}, bf16[640,768]{0,1:T(8,128)(2,1)S(1)}, u32[]{:S(2)}) copy-start(bf16[640,768]{0,1:T(8,128)(2,1)S(1)} %copy.172) | copy-start | bytes 2949124
  122.3 10.4 copy-start.29
  124.2 8.5 copy-start.13
  132.7 9.3 copy-start.60
  132.7 19.7 %slice-start = ((s8[4718592]{0:T(1024)(128)(4,1)}), s8[524288]{0:T(1024)(128)(4,1)S(1)}, s32[]{:S(2)}) async-start(s8[4718592]{0:T(1024)(128)(4,1)} %bitcast.313), calls=%async_computation.8 | async-start | bytes 1048576
  142.0 8.7 copy-start.77
  142.1 8.7 copy-start.16
  142.1 8.7 copy-start.138
  142.1 10.4 slice-start.1
  150.8 23.5 %slice-start.8 = ((s8[4718592]{0:T(1024)(128)(4,1)}), s8[4194304]{0:T(1024)(128)(4,1)S(1)}, s32[]{:S(2)}) async-start(s8[4718592]{0:T(1024)(128)(4,1)} %bitcast.325), calls=%async_computation.16 | async-start | bytes 8388608
  152.1 22.3 %copy-start.6 = (f32[640,768]{1,0:T(8,128)}, f32[640,768]{1,0:T(8,128)S(1)}, u32[]{:S(2)}) copy-start(f32[640,768]{1,0:T(8,128)S(1)} %get-tuple-element.862) | copy-start | bytes 5898244
  152.1 22.2 %copy-start.64 = (f32[640]{0:T(1024)}, f32[640]{0:T(1024)S(1)}, u32[]{:S(2)}) copy-start(f32[640]{0:T(1024)S(1)} %broadcast_multiply_fusion.16) | copy-start | bytes 7684
  152.5 21.9 %copy-start.67 = (f32[640]{0:T(1024)}, f32[640]{0:T(1024)S(1)}, u32[]{:S(2)}) copy-start(f32[640]{0:T(1024)S(1)} %add_rsqrt_fusion.4) | copy-start | bytes 7684
  152.5 21.8 %slice-start.9 = ((s8[4718592]{0:T(1024)(128)(4,1)}), s8[524288]{0:T(1024)(128)(4,1)S(1)}, s32[]{:S(2)}) async-start(s8[4718592]{0:T(1024)(128)(4,1)} %bitcast.325), calls=%async_computation.17 | async-start | bytes 1048576
  174.4 8.2 copy-start.82
  177.7 3.5 collective-permute-start.1
  204.6 26.4 %copy-start.61 = (f32[12,640]{1,0:T(8,128)S(1)}, f32[12,640]{1,0:T(8,128)}, u32[]{:S(2)}) copy-start(f32[12,640]{1,0:T(8,128)} %copy-done.60) | copy-start | bytes 92164
  204.6 26.4 %copy-start.78 = (f32[12,640]{1,0:T(8,128)S(1)}, f32[12,640]{1,0:T(8,128)}, u32[]{:S(2)}) copy-start(f32[12,640]{1,0:T(8,128)} %copy-done.77) | copy-start | bytes 92164
  204.6 231.0 %copy-start.107 = (f32[640]{0:T(1024)S(1)}, f32[640]{0:T(1024)}, u32[]{:S(2)}) copy-start(f32[640]{0:T(1024)} %copy-done.106) | copy-start | bytes 7684
  229.7 217.8 %copy-start.86 = (f32[3072]{0:T(1024)}, f32[3072]{0:T(1024)S(1)}, u32[]{:S(2)}) copy-start(f32[3072]{0:T(1024)S(1)} %get-tuple-element.412) | copy-start | bytes 36868
  229.7 217.8 %copy-start.90 = (f32[1536]{0:T(1024)}, f32[1536]{0:T(1024)S(1)}, u32[]{:S(2)}) copy-start(f32[1536]{0:T(1024)S(1)} %get-tuple-element.400) | copy-start | bytes 18436
  229.7 217.8 %copy-start.109 = (f32[768]{0:T(1024)}, f32[768]{0:T(1024)S(1)}, u32[]{:S(2)}) copy-start(f32[768]{0:T(1024)S(1)} %get-tuple-element.394) | copy-start | bytes 9220
  229.7 217.8 %copy-start.111 = (f32[768]{0:T(1024)}, f32[768]{0:T(1024)S(1)}, u32[]{:S(2)}) copy-start(f32[768]{0:T(1024)S(1)} %get-tuple-element.396) | copy-start | bytes 9220
  229.7 217.8 %copy-start.113 = (f32[768]{0:T(1024)}, f32[768]{0:T(1024)S(1)}, u32[]{:S(2)}) copy-start(f32[768]{0:T(1024)S(1)} %get-tuple-element.404) | copy-start | bytes 9220
  229.7 217.8 %copy-start.115 = (f32[768]{0:T(1024)}, f32[768]{0:T(1024)S(1)}, u32[]{:S(2)}) copy-start(f32[768]{0:T(1024)S(1)} %get-tuple-element.406) | copy-start | bytes 9220
  229.7 217.8 %copy-start.117 = (f32[768]{0:T(1024)}, f32[768]{0:T(1024)S(1)}, u32[]{:S(2)}) copy-start(f32[768]{0:T(1024)S(1)} %get-tuple-element.408) | copy-start | bytes 9220
  229.7 217.8 %copy-start.119 = (f32[768]{0:T(1024)}, f32[768]{0:T(1024)S(1)}, u32[]{:S(2)}) copy-start(f32[768]{0:T(1024)S(1)} %get-tuple-element.416) | copy-start | bytes 9220
  229.7 205.9 %collective-permute-start.2 = (bf16[640,768]{1,0:T(8,128)(2,1)}, bf16[640,768]{1,0:T(8,128)(2,1)S(1)}, u32[]{:S(2)}, u32[]{:S(2)}) collective-permute-start(bf16[640,768]{1,0:T(8,128)(2,1)} %get-tuple-element.380), channel_id=1, source_target_pairs={{16,0},{17,1},{18,2},{19,3},{20,4},{21,5},{22,6},{23,7},{24,8},{25... | collective-permute-start | bytes 2949128 | tf_op jit(solution)/shard_map/ppermute | solution.py:18
  435.6 11.9 slice-start.2
  438.0 9.5 copy-start.44
  438.0 9.6 copy-start.7
  438.0 9.6 copy-start.65
  438.0 9.6 copy-start.68
  438.0 9.6 copy-start.71
  438.0 9.6 slice-start.3
  458.2 11.0 copy-start.31
  509.7 4.6 collective-permute-start.3
  516.4 9.3 slice-start.6
  516.7 9.0 copy-start.40
  516.7 9.0 slice-start.7
  642.0 9.7 copy-start.41
  674.4 287.0 %reduce-scatter.5.cloned.1.call-start = ((), (), s32[]{:S(2)}) async-start(), calls=%async_computation.4 | async-start | bytes 7520256 | tf_op jit(solution)/shard_map/reduce_scatter | solution.py:262
  691.4 446.3 %reduce-scatter.9.cloned.1.call-start = ((), (), s32[]{:S(2)}) async-start(), calls=%async_computation.6 | async-start | bytes 10027008 | tf_op jit(solution)/shard_map/reduce_scatter | solution.py:268
  706.8 606.8 %reduce-scatter.11.cloned.1.call-start = ((), (), s32[]{:S(2)}) async-start(), calls=%async_computation.7 | async-start | bytes 10027008 | tf_op jit(solution)/shard_map/reduce_scatter | solution.py:270
  727.6 85.8 %copy-start.32 = (bf16[1,1,640,768]{3,2,1,0:T(8,128)(2,1)S(1)}, bf16[1,1,640,768]{3,2,1,0:T(8,128)(2,1)}, u32[]{:S(2)}) copy-start(bf16[1,1,640,768]{3,2,1,0:T(8,128)(2,1)} %get-tuple-element.807) | copy-start | bytes 2949124
  727.6 85.8 %copy-start.37 = (bf16[1,1,640,768]{3,2,1,0:T(8,128)(2,1)S(1)}, bf16[1,1,640,768]{3,2,1,0:T(8,128)(2,1)}, u32[]{:S(2)}) copy-start(bf16[1,1,640,768]{3,2,1,0:T(8,128)(2,1)} %get-tuple-element.853) | copy-start | bytes 2949124
  (83 other events, 357.2 us)
Sparse Core Ops, SparseCore 0:
  674.5 130.3 reduce-scatter.6
  811.7 149.6 reduce-scatter.4
  968.6 169.0 reduce-scatter.8
  1143.8 169.7 reduce-scatter.10
where the time goes:
time: 1330 us; the launch traced here: 1320 us
  waiting for transfers between devices  704 us (53%)
  matrix products  281 us (21%)
  other arithmetic  124 us (9%)
  local copies, waits for them, and re-layouts  91.6 us (7%)
  blocking collectives  79 us (6%)
  between operations  17.8 us (1%)
  loops' own time  16.9 us (1%)
    ppermute x4, waiting for transfers between devices, passed_along(): return lax.ppermute(block, axis, route)  207 us
    reduce_scatter x1, waiting for transfers between devices, sum_once(): lax.psum_scatter(w_up, 'dp', scatter_dimension=0, tiled=True)  176 us
    reduce_scatter x1, waiting for transfers between devices, sum_once(): lax.psum_scatter(w_down, 'dp', scatter_dimension=0, tiled=True)  176 us
    reduce_scatter x1, waiting for transfers between devices, sum_once(): lax.psum_scatter(w_qkv, 'dp', scatter_dimension=0, tiled=True)  145 us
    unnamed x1, blocking collectives  79 us
    dot_general x2, matrix products, forward_layer(): jnp.dot(second_low, w_up, preferred_element_type=jnp.float32) + bias_up  44.6 us
    dot_general x3, matrix products, attention_scores(): jnp.einsum('qhd,khd->hqk', queries, keys, preferred_element_type=jnp.floa...  30.5 us
    another operation x28, local copies, waits for them, and re-layouts  29.7 us
  transfers between devices with their start and end apart: 8, of which 6 were waited for; matrix products, arithmetic and copies ran while one was open for 5% of the time, Pallas kernels for 0%

commit v1 on v0

v1 whole, which is shorter than its diff:
```python
import functools
import jax
import jax.numpy as jnp
from jax import lax
from jax.experimental import pallas as pl
from jax.experimental.pallas import tpu as pltpu
from jax.sharding import PartitionSpec as P

HEAD_DIM = 64
LANES = 128
keep_rate = 0.9
norm_eps = 1e-06
root_half = 0.7071067811865476
inverse_root = 0.3989422804014327
BIG = 2.0**30
f32, bf16 = jnp.float32, jnp.bfloat16
NN = (((1,), (0,)), ((), ()))
NT = (((1,), (1,)), ((), ()))
TN = (((0,), (0,)), ((), ()))


def dot(a, b, dims=NN):
    return lax.dot_general(a, b, dims, preferred_element_type=f32)


def layer_unit(x):
    center = x - jnp.mean(x, axis=-1, keepdims=True)
    scale = lax.rsqrt(jnp.mean(center * center, axis=-1, keepdims=True) + norm_eps)
    return center * scale, scale


def unit_back(grad, unit, scale, gain):
    scaled = grad * gain
    inner = jnp.mean(scaled, axis=-1, keepdims=True)
    along = jnp.mean(scaled * unit, axis=-1, keepdims=True)
    return scale * (scaled - inner - unit * along)


def gelu_pair(h):
    e = jnp.exp(h * h * -0.5)
    t = 1.0 / (jnp.abs(h) * (0.3275911 * root_half) + 1.0)
    poly = t * (0.5 * 0.254829592 + t * (0.5 * -0.284496736 + t * (0.5 * 1.421413741 + t * (0.5 * -1.453152027 + t * (0.5 * 1.061405429)))))
    tail = poly * e
    phi = jnp.where(h < 0, tail, 1.0 - tail)
    return h * phi, phi + h * e * inverse_root


def split3(v):
    a = v.astype(bf16)
    r = v - a.astype(f32)
    b = r.astype(bf16)
    c = (r - b.astype(f32)).astype(bf16)
    return a, b, c


def feature_base(odd):
    return 0 if odd else HEAD_DIM


def lanes_of(rows):
    return lax.broadcasted_iota(jnp.int32, (rows, LANES), 1)


def seg_feature(seg, rows, odd):
    base = feature_base(odd)
    lane = lanes_of(rows)
    inside = (lane >= base) & (lane < base + 8)
    same = (lane - base).astype(f32) == seg
    qf = jnp.where(inside & same, BIG, 0.0)
    kf = jnp.where(inside & jnp.logical_not(same), -1.0, 0.0)
    kf = jnp.where((lane >= base + 8) & (lane < base + 11), 1.0, kf)
    return qf.astype(bf16), kf.astype(bf16)


def own_lanes(rows, odd):
    lane = lanes_of(rows)
    return (lane >= HEAD_DIM) if odd else (lane < HEAD_DIM)


def forward_kernel(l, x_ref, cols_ref, par_ref, wqkv_ref, wo_ref, w1_ref, w2_ref,
                   y_ref, qkv_ref, lse_ref, att_ref, mid_ref, act_ref, slope_ref,
                   norm_s, second_s, feat_s):
    T, D = x_ref.shape
    FF = w1_ref.shape[1]
    W = 256

    RC = 128

    @pl.loop(0, T // RC)
    def _(i):
        rows = pl.ds(i * RC, RC)
        unit, _s = layer_unit(x_ref[rows, :].astype(f32))
        norm_s[rows, :] = (unit * par_ref[0:1, :D] + par_ref[1:2, :D]).astype(bf16)
        for odd in (0, 1):
            qf, kf = seg_feature(cols_ref[rows, 0:1], RC, odd)
            feat_s[2 * odd, rows, :] = qf
            feat_s[2 * odd + 1, rows, :] = kf

    @pl.loop(0, 3 * D // W)
    def _(n):
        cs = pl.ds(pl.multiple_of(n * W, W), W)
        acc = dot(norm_s[...], wqkv_ref[:, cs]) + par_ref[2:3, cs]
        qkv_ref[:, cs] = (acc * jnp.where(n < D // W, 0.125, 1.0)).astype(bf16)

    heads2 = D // LANES

    @pl.loop(0, heads2)
    def _(p):
        off = pl.multiple_of(p * LANES, LANES)
        qp = qkv_ref[:, pl.ds(off, LANES)]
        kp = qkv_ref[:, pl.ds(off + D, LANES)]
        vp = qkv_ref[:, pl.ds(off + 2 * D, LANES)]
        outs = []
        for odd in (0, 1):
            own = own_lanes(T, odd)
            base = feature_base(odd)
            q = jnp.where(own, qp, feat_s[2 * odd])
            k = jnp.where(own, kp, feat_s[2 * odd + 1])
            v = jnp.where(own, vp, jnp.ones_like(vp))
            s = dot(q, k, NT)
            m = jnp.max(s, axis=1, keepdims=True)
            e = jnp.exp(s - m).astype(bf16)
            o = dot(e, v)
            total = o[:, base:base + 1]
            outs.append(o / total)
            lse_ref[p, :, odd:odd + 1] = m + jnp.log(total)
        att_ref[:, pl.ds(off, LANES)] = jnp.where(own_lanes(T, 0), outs[0], outs[1]).astype(bf16)

    @pl.loop(0, D // W)
    def _(n):
        cs = pl.ds(pl.multiple_of(n * W, W), W)
        acc = dot(att_ref[...], wo_ref[:, cs]) + par_ref[3:4, cs]
        mid_ref[:, cs] = x_ref[:, cs].astype(f32) + cols_ref[:, 1 + 2 * l:2 + 2 * l] * acc

    @pl.loop(0, T // RC)
    def _(i):
        rows = pl.ds(i * RC, RC)
        unit, _s = layer_unit(mid_ref[rows, :])
        second_s[rows, :] = (unit * par_ref[4:5, :D] + par_ref[5:6, :D]).astype(bf16)

    @pl.loop(0, FF // W)
    def _(n):
        cs = pl.ds(pl.multiple_of(n * W, W), W)
        h = dot(second_s[...], w1_ref[:, cs]) + par_ref[6:7, cs]
        a, s = gelu_pair(h)
        act_ref[:, cs] = a.astype(bf16)
        slope_ref[:, cs] = s.astype(bf16)

    @pl.loop(0, D // W)
    def _(n):
        cs = pl.ds(pl.multiple_of(n * W, W), W)
        acc = dot(act_ref[...], w2_ref[:, cs]) + par_ref[7:8, cs]
        y_ref[:, cs] = (mid_ref[:, cs] + cols_ref[:, 2 + 2 * l:3 + 2 * l] * acc).astype(bf16)


VM = pl.BlockSpec(memory_space=pltpu.VMEM)
LIMIT = 60 * 2**20


def forward_call(l, x, cols, par, wqkv, wo, w1, w2):
    T, D = x.shape
    FF = w1.shape[1]
    sd = jax.ShapeDtypeStruct
    return pl.pallas_call(
        functools.partial(forward_kernel, l),
        out_shape=(sd((T, D), bf16), sd((T, 3 * D), bf16), sd((D // LANES, T, 2), f32), sd((T, D), bf16),
                   sd((T, D), f32), sd((T, FF), bf16), sd((T, FF), bf16)),
        in_specs=[VM] * 7, out_specs=(VM,) * 7,
        scratch_shapes=[pltpu.VMEM((T, D), bf16), pltpu.VMEM((T, D), bf16), pltpu.VMEM((4, T, LANES), bf16)],
        compiler_params=pltpu.CompilerParams(vmem_limit_bytes=LIMIT), name="fwd_layer",
    )(x, cols, par, wqkv, wo, w1, w2)


def mlp_back_kernel(l, g_ref, cols_ref, par_ref, mid_ref, act_ref, slope_ref, w1_ref, w2_ref,
                    gmid_ref, dw1_ref, dw2_ref, vec_ref, gd_s, second_s, gh_s, gs_s):
    T, D = g_ref.shape
    FF = w1_ref.shape[1]
    W = 256
    RC = 128
    vec_ref[...] = jnp.zeros_like(vec_ref)

    @pl.loop(0, T // RC)
    def _(i):
        rows = pl.ds(i * RC, RC)
        gd = (g_ref[rows, :].astype(f32) * cols_ref[rows, 2 + 2 * l:3 + 2 * l]).astype(bf16)
        gd_s[rows, :] = gd
        vec_ref[3:4, :D] += jnp.sum(gd.astype(f32), axis=0, keepdims=True)
        unit, _s = layer_unit(mid_ref[rows, :])
        second_s[rows, :] = (unit * par_ref[4:5, :D] + par_ref[5:6, :D]).astype(bf16)

    shard1 = dw1_ref.shape[2]
    per_half = dw1_ref.shape[3] // W

    @pl.loop(0, FF // W)
    def _(n):
        cs = pl.ds(pl.multiple_of(n * W, W), W)
        ga = dot(gd_s[...], w2_ref[cs, :], NT)
        gh = (ga * slope_ref[:, cs].astype(f32)).astype(bf16)
        gh_s[:, cs] = gh
        vec_ref[2:3, cs] = jnp.sum(gh.astype(f32), axis=0, keepdims=True)
        d1 = dot(second_s[...], gh, TN).astype(bf16)
        dw1_ref[n // per_half, :, :, pl.ds(pl.multiple_of((n % per_half) * W, W), W)] = d1.reshape(-1, shard1, W)
        d2 = dot(act_ref[:, cs], gd_s[...], TN).astype(bf16)
        dw2_ref[0, cs, :] = d2[:, :D // 2]
        dw2_ref[1, cs, :] = d2[:, D // 2:]

    @pl.loop(0, D // W)
    def _(n):
        cs = pl.ds(pl.multiple_of(n * W, W), W)
        gs_s[:, cs] = dot(gh_s[...], w1_ref[cs, :], NT)

    @pl.loop(0, T // RC)
    def _(i):
        rows = pl.ds(i * RC, RC)
        unit, scale = layer_unit(mid_ref[rows, :])
        gs = gs_s[rows, :]
        vec_ref[0:1, :D] += jnp.sum(gs * unit, axis=0, keepdims=True)
        vec_ref[1:2, :D] += jnp.sum(gs, axis=0, keepdims=True)
        gmid_ref[rows, :] = g_ref[rows, :].astype(f32) + unit_back(gs, unit, scale, par_ref[4:5, :D])


def mlp_back_call(l, n_dp, g, cols, par, mid, act, slope, w1, w2):
    T, D = g.shape
    FF = w1.shape[1]
    sd = jax.ShapeDtypeStruct
    return pl.pallas_call(
        functools.partial(mlp_back_kernel, l),
        out_shape=(sd((T, D), f32), sd((2, n_dp, D // n_dp, FF // 2), bf16), sd((2, FF, D // 2), bf16), sd((8, FF), f32)),
        in_specs=[VM] * 8, out_specs=(VM,) * 4,
        scratch_shapes=[pltpu.VMEM((T, D), bf16), pltpu.VMEM((T, D), bf16), pltpu.VMEM((T, FF), bf16), pltpu.VMEM((T, D), f32)],
        compiler_params=pltpu.CompilerParams(vmem_limit_bytes=LIMIT), name="mlp_back",
    )(g, cols, par, mid, act, slope, w1, w2)


def attn_back_kernel(l, gmid_ref, cols_ref, par_ref, x_ref, qkv_ref, lse_ref, att_ref, wqkv_ref, wo_ref,
                     gin_ref, dqkv_ref, dwo_ref, vec_ref, gb_s, norm_s, ga_s, gm_s, feat_s, gn_s):
    T, D = x_ref.shape
    W = 256
    RC = 128
    vec_ref[...] = jnp.zeros_like(vec_ref)

    @pl.loop(0, T // RC)
    def _(i):
        rows = pl.ds(i * RC, RC)
        gb = (gmid_ref[rows, :] * cols_ref[rows, 1 + 2 * l:2 + 2 * l]).astype(bf16)
        gb_s[rows, :] = gb
        vec_ref[3:4, :D] += jnp.sum(gb.astype(f32), axis=0, keepdims=True)
        unit, _s = layer_unit(x_ref[rows, :].astype(f32))
        norm_s[rows, :] = (unit * par_ref[0:1, :D] + par_ref[1:2, :D]).astype(bf16)
        for odd in (0, 1):
            qf, kf = seg_feature(cols_ref[rows, 0:1], RC, odd)
            feat_s[2 * odd, rows, :] = qf
            feat_s[2 * odd + 1, rows, :] = kf

    @pl.loop(0, D // W)
    def _(n):
        cs = pl.ds(pl.multiple_of(n * W, W), W)
        ga_s[:, cs] = dot(gb_s[...], wo_ref[cs, :], NT).astype(bf16)

    heads2 = D // LANES
    low_lane = own_lanes(T, 0)

    @pl.loop(0, heads2)
    def _(p):
        off = pl.multiple_of(p * LANES, LANES)
        qp = qkv_ref[:, pl.ds(off, LANES)]
        kp = qkv_ref[:, pl.ds(off + D, LANES)]
        vp = qkv_ref[:, pl.ds(off + 2 * D, LANES)]
        gp = ga_s[:, pl.ds(off, LANES)]
        prod = gp.astype(f32) * att_ref[:, pl.ds(off, LANES)].astype(f32)
        dq, dk, dv = [], [], []
        for odd in (0, 1):
            own = own_lanes(T, odd)
            base = feature_base(odd)
            lane = lanes_of(T)
            row_d = jnp.sum(jnp.where(own, prod, 0.0), axis=1, keepdims=True)
            l3 = split3(-lse_ref[p, :, odd:odd + 1])
            d3 = split3(-row_d)
            qf = feat_s[2 * odd]
            gf = jnp.zeros_like(gp)
            for j in range(3):
                qf = jnp.where(lane == base + 8 + j, l3[j], qf)
                gf = jnp.where(lane == base + j, d3[j], gf)
            q = jnp.where(own, qp, qf)
            k = jnp.where(own, kp, feat_s[2 * odd + 1])
            v = jnp.where(own, vp, jnp.ones_like(vp))
            g = jnp.where(own, gp, gf)
            prob = jnp.exp(dot(k, q, NT))
            gs = (prob * dot(v, g, NT)).astype(bf16)
            dv.append(dot(prob.astype(bf16), g))
            dk.append(dot(gs, q))
            dq.append(dot(gs, k, TN))
        gm_s[:, pl.ds(off, LANES)] = (jnp.where(low_lane, dq[0], dq[1]) * 0.125).astype(bf16)
        gm_s[:, pl.ds(off + D, LANES)] = jnp.where(low_lane, dk[0], dk[1]).astype(bf16)
        gm_s[:, pl.ds(off + 2 * D, LANES)] = jnp.where(low_lane, dv[0], dv[1]).astype(bf16)

    shard = dwo_ref.shape[2]

    @pl.loop(0, D // LANES)
    def _(n):
        half = n // (D // LANES // 2)
        o = pl.multiple_of(n * LANES, LANES)
        ho = pl.multiple_of((n % (D // LANES // 2)) * LANES, LANES)
        dwo_ref[half, :, :, pl.ds(ho, LANES)] = dot(att_ref[...], gb_s[:, pl.ds(o, LANES)], TN).astype(bf16).reshape(-1, shard, LANES)

    W3 = 3 * D // 6

    @pl.loop(0, 6)
    def _(n):
        o = pl.multiple_of(n * W3, LANES)
        ho = pl.multiple_of((n % 3) * W3, LANES)
        gm = gm_s[:, pl.ds(o, W3)]
        dqkv_ref[n // 3, :, :, pl.ds(ho, W3)] = dot(norm_s[...], gm, TN).astype(bf16).reshape(-1, shard, W3)
        vec_ref[2:3, pl.ds(o, W3)] = jnp.sum(gm.astype(f32), axis=0, keepdims=True)

    @pl.loop(0, D // W)
    def _(n):
        cs = pl.ds(pl.multiple_of(n * W, W), W)
        gn_s[:, cs] = dot(gm_s[...], wqkv_ref[cs, :], NT)

    @pl.loop(0, T // RC)
    def _(i):
        rows = pl.ds(i * RC, RC)
        unit, scale = layer_unit(x_ref[rows, :].astype(f32))
        gn = gn_s[rows, :]
        vec_ref[0:1, :D] += jnp.sum(gn * unit, axis=0, keepdims=True)
        vec_ref[1:2, :D] += jnp.sum(gn, axis=0, keepdims=True)
        gin_ref[rows, :] = (gmid_ref[rows, :] + unit_back(gn, unit, scale, par_ref[0:1, :D])).astype(bf16)


def attn_back_call(l, n_dp, gmid, cols, par, x, qkv, lse, att, wqkv, wo):
    T, D = x.shape
    sd = jax.ShapeDtypeStruct
    return pl.pallas_call(
        functools.partial(attn_back_kernel, l),
        out_shape=(sd((T, D), bf16), sd((2, n_dp, D // n_dp, 3 * D // 2), bf16), sd((2, n_dp, D // n_dp, D // 2), bf16), sd((8, 4 * D), f32)),
        in_specs=[VM] * 9, out_specs=(VM,) * 4,
        scratch_shapes=[pltpu.VMEM((T, D), bf16), pltpu.VMEM((T, D), bf16), pltpu.VMEM((T, D), bf16), pltpu.VMEM((T, 3 * D), bf16),
                        pltpu.VMEM((4, T, LANES), bf16), pltpu.VMEM((T, D), f32)],
        compiler_params=pltpu.CompilerParams(vmem_limit_bytes=LIMIT), name="attn_back",
    )(gmid, cols, par, x, qkv, lse, att, wqkv, wo)


MESH = pl.DeviceIdType.MESH
ANY = pl.BlockSpec(memory_space=pl.ANY)


def peers(X, Y, Z):
    me = lax.axis_index("dp")
    mx, my, mz = me % X, (me // X) % Y, me // (X * Y)
    return me, mx, my, mz


def greet(X, Y, Z):
    me, mx, my, mz = peers(X, Y, Z)
    sec = lax.axis_index("section")
    bar = pltpu.get_barrier_semaphore()
    ids = [{"section": 1 - sec}, {"dp": me + 1 - 2 * mx}, {"dp": me + X * (1 - 2 * my)}]
    ids += [{"dp": lax.rem(mz + j, Z) * (X * Y) + me % (X * Y)} for j in range(1, Z)]
    for i in ids:
        pl.semaphore_signal(bar, inc=1, device_id=i, device_id_type=MESH)
    pl.semaphore_wait(bar, len(ids))


def swap_kernel(n, *refs):
    mine, theirs, send, recv = refs[:n], refs[n:2 * n], refs[2 * n], refs[2 * n + 1]
    other = {"section": 1 - lax.axis_index("section")}
    bar = pltpu.get_barrier_semaphore()
    pl.semaphore_signal(bar, inc=1, device_id=other, device_id_type=MESH)
    pl.semaphore_wait(bar, 1)
    copies = [
        pltpu.make_async_remote_copy(mine[i], theirs[i], send.at[i], recv.at[i], device_id=other, device_id_type=MESH)
        for i in range(n)
    ]
    for c in copies:
        c.start()
    for c in copies:
        c.wait()


def swap_call(arrays):
    n = len(arrays)
    return pl.pallas_call(
        functools.partial(swap_kernel, n),
        out_shape=tuple(jax.ShapeDtypeStruct(a.shape, a.dtype) for a in arrays),
        in_specs=[ANY] * n, out_specs=(ANY,) * n,
        scratch_shapes=[pltpu.SemaphoreType.DMA((n,)), pltpu.SemaphoreType.DMA((n,))],
        compiler_params=pltpu.CompilerParams(collective_id=0, has_side_effects=True), name="swap_weights",
    )(*arrays)


def reduce_kernel(dims, units, n_src, n_out, *refs):
    X, Y, Z = dims
    N = len(units)
    srcs, outs = refs[:n_src], refs[n_src:n_src + n_out]
    rest = refs[n_src + n_out:]
    own, r0, r1, r2, r3, fin = (rest[i * N:(i + 1) * N] for i in range(6))
    send, recv, lsem = rest[6 * N:]
    sec = lax.axis_index("section")
    me, mx, my, mz = peers(X, Y, Z)
    other = {"section": 1 - sec}
    greet(X, Y, Z)

    def remote(u, k, src, dst, dev):
        return pltpu.make_async_remote_copy(src, dst, send.at[u, k], recv.at[u, k], device_id=dev, device_id_type=MESH)

    def view(u, half):
        src, row, rows, col, cols = units[u][:5]
        return srcs[src].at[half, :, :, :, pl.ds(row, rows), pl.ds(col, cols)]

    loads = [pltpu.make_async_copy(view(u, sec), own[u], lsem.at[u]) for u in range(N)]
    c0 = [remote(u, 0, view(u, 1 - sec), r0[u], other) for u in range(N)]
    for u in range(N):
        c0[u].start()
        loads[u].start()

    def stage1(u):
        loads[u].wait()
        c0[u].wait()
        dt = own[u].dtype

        @pl.loop(0, Z)
        def _(z):
            for y in range(Y):
                for x in range(X):
                    own[u][z, y, x] = (own[u][z, y, x].astype(f32) + r0[u][z, y, x].astype(f32)).astype(dt)
        if units[u][5] == "xy":
            c = remote(u, 1, own[u].at[:, :, 1 - mx], r1[u], {"dp": me + 1 - 2 * mx})
        else:
            c = remote(u, 1, own[u].at[:, 1 - my], r1[u], {"dp": me + X * (1 - 2 * my)})
        c.start()
        return [c]

    def stage2(u, pend):
        pend[0].wait()
        dt = own[u].dtype

        @pl.loop(0, Z)
        def _(z):
            for w in range(2):
                y, x = (w, mx) if units[u][5] == "xy" else (my, w)
                own[u][z, y, x] = (own[u][z, y, x].astype(f32) + r1[u][z, w].astype(f32)).astype(dt)
        if units[u][5] == "xy":
            c = remote(u, 2, own[u].at[:, 1 - my, mx], r2[u], {"dp": me + X * (1 - 2 * my)})
        else:
            c = remote(u, 2, own[u].at[:, my, 1 - mx], r2[u], {"dp": me + 1 - 2 * mx})
        c.start()
        return [c]

    def stage3(u, pend):
        pend[0].wait()
        dt = own[u].dtype

        @pl.loop(0, Z)
        def _(z):
            own[u][z, my, mx] = (own[u][z, my, mx].astype(f32) + r2[u][z].astype(f32)).astype(dt)
        cs = []
        for j in range(1, Z):
            to = lax.rem(mz + j, Z)
            c = remote(u, 2 + j, own[u].at[to, my, mx], r3[u].at[j - 1], {"dp": to * (X * Y) + me % (X * Y)})
            c.start()
            cs.append(c)
        return cs

    def stage4(u, pend):
        for c in pend:
            c.wait()
        total = own[u][mz, my, mx].astype(f32)
        for j in range(1, Z):
            total += r3[u][j - 1].astype(f32)
        fin[u][...] = total

    pend = {}
    for step in range(N + 3):
        for u, fn in ((step, stage1), (step - 1, stage2), (step - 2, stage3), (step - 3, stage4)):
            if 0 <= u < N:
                pend[u] = fn(u) if fn is stage1 else fn(u, pend[u])
    last = []
    for u in range(N):
        layer, out, row, rows, col, cols, width = units[u][6:]
        if layer is None:
            c = pltpu.make_async_copy(fin[u], outs[out], lsem.at[u])
            c.start()
            c.wait()
            continue
        dst = outs[out].at[pl.ds(row, rows), pl.ds(pl.multiple_of(sec * width + col, LANES), cols)]
        local = pltpu.make_async_copy(fin[u], dst, lsem.at[u])
        away = remote(u, Z + 2, fin[u], dst, other)

        @pl.when(sec == layer)
        def _():
            local.start()

        @pl.when(sec != layer)
        def _():
            away.start()
        last.append((layer, local, away))
    for layer, local, away in last:
        @pl.when(sec == layer)
        def _():
            local.wait()
            away.wait_recv()

        @pl.when(sec != layer)
        def _():
            away.wait_send()


def reduce_call(dims, srcs, units, outs, cid):
    X, Y, Z = dims
    N = len(units)
    dts = [srcs[u[0]].dtype for u in units]
    shp = [(u[2], u[4]) for u in units]
    scr = [pltpu.VMEM((Z, Y, X) + s, d) for s, d in zip(shp, dts)] * 2
    scr += [pltpu.VMEM((Z, 2) + s, d) for s, d in zip(shp, dts)]
    scr += [pltpu.VMEM((Z,) + s, d) for s, d in zip(shp, dts)]
    scr += [pltpu.VMEM((Z - 1,) + s, d) for s, d in zip(shp, dts)]
    scr += [pltpu.VMEM(s, f32) for s in shp]
    scr += [pltpu.SemaphoreType.DMA((N, Z + 3)), pltpu.SemaphoreType.DMA((N, Z + 3)), pltpu.SemaphoreType.DMA((N,))]
    return pl.pallas_call(
        functools.partial(reduce_kernel, dims, units, len(srcs), len(outs)),
        out_shape=tuple(jax.ShapeDtypeStruct(o, f32) for o in outs),
        in_specs=[ANY] * len(srcs), out_specs=(ANY,) * len(outs), scratch_shapes=scr,
        compiler_params=pltpu.CompilerParams(collective_id=cid, has_side_effects=True, vmem_limit_bytes=LIMIT), name="reduce_grads",
    )(*srcs)


def dp_dims(n):
    return {16: (2, 2, 4)}.get(n)


def shards(
    tokens, segment_ids, keep_masks, cotangent,
    norm1_gain, norm1_bias, qkv_weight, qv_bias, out_weight, out_bias,
    norm2_gain, norm2_bias, fc1_weight, fc1_bias, fc2_weight, fc2_bias,
):
    sec = lax.axis_index("section")
    n_dp = lax.axis_size("dp")
    dims = dp_dims(n_dp)
    T, D = tokens.shape[1:]
    FF = fc1_weight.shape[2]
    pad = lambda v: jnp.pad(v, (0, FF - v.shape[0]))
    bq = jnp.concatenate([qv_bias[0, :D], jnp.zeros((D,), f32), qv_bias[0, D:]])
    par = jnp.stack([pad(v) for v in (norm1_gain[0], norm1_bias[0], bq, out_bias[0], norm2_gain[0], norm2_bias[0], fc1_bias[0], fc2_bias[0])])
    keep = jnp.pad(keep_masks[0].astype(f32).reshape(4, -1), ((0, 4), (0, LANES - keep_masks.shape[3])))
    own = (qkv_weight[0], out_weight[0], fc1_weight[0], fc2_weight[0], par, keep)
    other = swap_call(own)
    layers = [[jnp.where(sec == l, a, b) for a, b in zip(own, other)] for l in range(2)]
    seg = lax.dynamic_index_in_dim(segment_ids, sec, 0, keepdims=False)
    onehot = (seg[:, None] == jnp.arange(LANES, dtype=jnp.int32)[None]).astype(f32)
    flags = []
    for l in range(2):
        table = lax.dynamic_slice_in_dim(layers[l][5], sec * 2, 2, 0)
        flags.append(jnp.sum(onehot[:, None, :] * table[None], axis=2) / keep_rate)
    cols = jnp.concatenate([seg[:, None].astype(f32)] + flags + [jnp.zeros((T, LANES - 5), f32)], axis=1)
    x = lax.dynamic_index_in_dim(tokens, sec, 0, keepdims=False)
    g = lax.dynamic_index_in_dim(cotangent, sec, 0, keepdims=False)
    saved, ys, gs, grads, vecs = [], [], [], [None, None], [None, None]
    for l in range(2):
        wqkv, wo, w1, w2, par_l, _ = layers[l]
        y, qkv, lse, att, mid, act, slope = forward_call(l, x, cols, par_l, wqkv, wo, w1, w2)
        saved.append((x, qkv, lse, att, mid, act, slope))
        x = y
        ys.append(y)
    for l in (1, 0):
        wqkv, wo, w1, w2, par_l, _ = layers[l]
        x, qkv, lse, att, mid, act, slope = saved[l]
        gmid, dw1, dw2, vm = mlp_back_call(l, n_dp, g, cols, par_l, mid, act, slope, w1, w2)
        g, dqkv, dwo, va = attn_back_call(l, n_dp, gmid, cols, par_l, x, qkv, lse, att, wqkv, wo)
        gs.append(g)
        grads[l] = (dqkv, dwo, dw1, dw2)
        parts = (va[0, :D], va[1, :D], jnp.concatenate([va[2, :D], va[2, 2 * D:3 * D]]), va[3, :D], vm[0, :D], vm[1, :D], vm[2], vm[3, :D])
        vecs[l] = jnp.concatenate([v.reshape(n_dp, -1) for v in parts], axis=1)
    mine = jnp.where(sec == 0, ys[0], ys[1]), jnp.where(sec == 0, gs[1], gs[0])
    away = jnp.where(sec == 0, ys[1], ys[0]), jnp.where(sec == 0, gs[0], gs[1])
    got = [lax.ppermute(a, "section", [(0, 1), (1, 0)]) for a in away]
    both = [jnp.where(sec == 0, jnp.stack([m, o]), jnp.stack([o, m]))[None] for m, o in zip(mine, got)]
    width = vecs[0].shape[1]
    vrows = -(-width // LANES)
    vrows = -(-vrows // 8) * 8
    vec = jnp.pad(jnp.stack(vecs), ((0, 0), (0, 0), (0, vrows * LANES - width)))
    if dims:
        X, Y, Z = dims
        srcs = [a.reshape(2, Z, Y, X, -1, a.shape[-1]) for l in (1, 0) for a in (grads[l][3], grads[l][2], grads[l][0], grads[l][1])]
        srcs.append(vec.reshape(2, Z, Y, X, vrows, LANES))
        units = []
        for i, l in enumerate((1, 0)):
            b = 4 * i
            r2, r = FF // n_dp, D // n_dp
            h2 = r2 // 2
            units += [
                (b, 0, h2, 0, D // 2, "xy", l, 3, 0, h2, 0, D // 2, D // 2),
                (b, h2, h2, 0, D // 2, "yx", l, 3, h2, h2, 0, D // 2, D // 2),
            ]
            for src, out, C, cut in ((1, 2, FF // 2, FF // 4), (2, 0, 3 * D // 2, 640), (3, 1, D // 2, 128)):
                units += [
                    (b + src, 0, r, 0, cut, "xy", l, out, 0, r, 0, cut, C),
                    (b + src, 0, r, cut, C - cut, "yx", l, out, 0, r, cut, C - cut, C),
                ]
        units.append((8, 0, vrows, 0, LANES, "xy", None, 4, 0, 0, 0, 0, 0))
        outs = [(D // n_dp, 3 * D), (D // n_dp, D), (D // n_dp, FF), (FF // n_dp, D), (vrows, LANES)]
        dqkv, dwo, dw1, dw2, v = reduce_call(dims, srcs, units, outs, 1)
        v = v.reshape(-1)
    else:
        full = [jnp.stack([jnp.concatenate([grads[l][i][0], grads[l][i][1]], axis=-1).astype(f32).reshape(n_dp, -1) for l in range(2)]) for i in range(4)]
        full.append(vec)
        res = []
        for a in full:
            a = lax.psum_scatter(a, "section", scatter_dimension=0, tiled=False)
            res.append(lax.psum_scatter(a, "dp", scatter_dimension=0, tiled=False))
        dqkv, dwo, dw1, dw2 = (a.reshape(-1, c) for a, c in zip(res, (3 * D, D, FF, D)))
        v = res[4].reshape(-1)
    d, f = D // n_dp, FF // n_dp
    cuts = [0, d, 2 * d, 4 * d, 5 * d, 6 * d, 7 * d, 7 * d + f, 8 * d + f]
    n1g, n1b, qv, ob, n2g, n2b, b1, b2 = (v[None, a:b] for a, b in zip(cuts[:-1], cuts[1:]))
    return (both[0], both[1], n1g, n1b, dqkv[None], qv, dwo[None], ob, n2g, n2b, dw1[None], b1, dw2[None], b2)


def solution(mesh):
    in_specs = (
        P(None, "dp", None), P(None, "dp"), P("section", None, None, "dp"), P(None, "dp", None),
        P("section", None), P("section", None), P("section", None, None), P("section", None),
        P("section", None, None), P("section", None), P("section", None), P("section", None),
        P("section", None, None), P("section", None), P("section", None, None), P("section", None),
    )
    out_specs = (
        P("section", None, "dp", None), P("section", None, "dp", None),
        P("section", "dp"), P("section", "dp"), P("section", "dp", None), P("section", "dp"),
        P("section", "dp", None), P("section", "dp"), P("section", "dp"), P("section", "dp"),
        P("section", "dp", None), P("section", "dp"), P("section", "dp", None), P("section", "dp"),
    )
    return jax.shard_map(shards, mesh=mesh, in_specs=in_specs, out_specs=out_specs, check_vma=False)
```

time: 1330 us -> 476 us (0.36)
  waiting for transfers between devices: 704 us -> 0.01 us
  Pallas kernels: 0 us -> 413 us
  matrix products: 281 us -> 0 us
  other arithmetic: 124 us -> 41 us
  blocking collectives: 79 us -> 0 us
  local copies, waits for them, and re-layouts: 91.6 us -> 19.8 us
  loops' own time: 16.9 us -> 0 us
  between operations: 17.8 us -> 0.98 us
    reduce_scatter x4 -> x0, waiting for transfers between devices: 497 us -> none  [the longest x1 176 us: sum_once(): lax.psum_scatter(w_up, 'dp', scatter_dimension=0, tiled=True)]
    pallas_call x0 -> x8, Pallas kernels: none -> 413 us  [the longest x1 157 us: reduce_call(): pl.pallas_call(functools.partial(reduce_kernel, dims, units, len(srcs), l...]
    dot_general x37 -> x0, matrix products: 281 us -> none  [the longest x2 44.6 us: forward_layer(): jnp.dot(second_low, w_up, preferred_element_type=jnp.float32) + bias_up]
    ppermute x4 -> x2, waiting for transfers between devices: 207 us -> 0.01 us  [shards(): got = [lax.ppermute(a, 'section', [(0, 1), (1, 0)]) for a in away]]
    unnamed x1 -> x0, blocking collectives: 79 us -> none
    convert_element_type x12 -> x3, other arithmetic: 37.9 us -> 0.86 us  [the longest x1 0.69 us: shards(): keep_masks[0].astype(f32).reshape(4, -1)]
    reduce_sum x16 -> x1, other arithmetic: 36.3 us -> 0.43 us  [shards(): flags.append(jnp.sum(onehot[:, None, :] * table[None], axis=2) / keep_rate)]
    cond x46 -> x0, local copies, waits for them, and re-layouts: 34.8 us -> none  [the longest x4 29.6 us: shards(): grad_input, piece = lax.cond(live, run_back, run_blank)]
  transfers between devices with their start and end apart: 8 -> 2, of which waited for: 6 -> 0; matrix products, arithmetic and copies ran while one was open for 5% -> 3% of each run, Pallas kernels for 0% -> 33%
where the time goes in v1:
time: 476 us; the launch traced here: 475 us
  Pallas kernels  413 us (87%)
  other arithmetic  41 us (9%)
  local copies, waits for them, and re-layouts  19.8 us (4%)
    pallas_call x1, Pallas kernels, reduce_call(): pl.pallas_call(functools.partial(reduce_kernel, dims, units, len(srcs), l...  157 us
    pallas_call x2, Pallas kernels, forward_call(): pl.pallas_call(functools.partial(forward_kernel, l), out_shape=(sd((T, D)...  84.5 us
    pallas_call x2, Pallas kernels, attn_back_call(): pl.pallas_call(functools.partial(attn_back_kernel, l), out_shape=(sd((T,...  75.4 us
    pallas_call x2, Pallas kernels, mlp_back_call(): pl.pallas_call(functools.partial(mlp_back_kernel, l), out_shape=(sd((T, D...  73.9 us
    select_n x6, other arithmetic, shards(): jnp.where(sec == l, a, b)  25.8 us
    pallas_call x1, Pallas kernels, swap_call(): pl.pallas_call(functools.partial(swap_kernel, n), out_shape=tuple((jax.Sh...  22.1 us
  transfers between devices with their start and end apart: 2, of which 0 were waited for; matrix products, arithmetic and copies ran while one was open for 3% of the time, Pallas kernels for 33%

profile of v1, /device:TPU:0, one launch (start us, length us, event | category | flops | bytes accessed | tf_op | source)
XLA Modules:
  0.0 475.4 jit_solution(14220290900668147859)
XLA Ops:
  0.7 0.9 slice_reduce_fusion.19
  1.5 0.7 reduce.5
  2.2 0.7 reduce.6
  3.0 0.7 reduce.7
  3.7 0.7 reduce.8
  4.4 0.7 reduce.1
  5.1 0.7 reduce.2
  5.8 0.7 convert_element_type.44
  6.5 0.6 pad.31.refs_5_
  7.1 1.5 stack.69.refs_4_
  8.6 22.1 %swap_weights.1 = (bf16[768,2304]{1,0:T(8,128)(2,1)}, bf16[768,768]{1,0:T(8,128)(2,1)}, bf16[768,3072]{1,0:T(8,128)(2,1)}, bf16[3072,768]{1,0:T(8,128)(2,1)}, f32[8,3072]{1,0:T(8,128)}, /*index=5*/f32[8,128]{1,0:T(8,128)}) custom-call(bf16[768,2304]{1,0:T(8,128)(2,1)} %bitcast.70, bf16[768,768]{1,0:T(8,128)(2,1)} %bitcast.75, bf16[768,3072]{1,0:T(8,128)(2,1)} %bitcast.67, ...), custom_call_target="tpu_custom_call" | custom-call | tf_op jit(solution)/shard_map/swap_weights/pallas_call | solution.py:383
  30.7 0.7 broadcast_select_fusion.12
  31.4 0.1 fusion
  31.6 0.4 multiply_reduce_fusion.1
  32.0 0.2 copy.37
  32.2 0.2 copy.38
  32.4 0.2 copy.36
  32.6 1.7 broadcast_select_fusion.10
  34.4 8.1 %broadcast_select_fusion = (bf16[3072,768]{1,0:T(8,128)(2,1)}, bf16[3072,768]{1,0:T(8,128)(2,1)}) fusion(bf16[3072,768]{1,0:T(8,128)(2,1)} %get-tuple-element.60, pred[]{:T(512)S(6)} %eq.21, bf16[1,3072,768]{2,1,0:T(8,128)(2,1)} %param.30, pred[]{:T(512)S(6)} %eq.16), kind=kLoop, calls=%fused_computation | loop fusion | flops 4718592 | bytes 18874370 | tf_op jit(solution)/shard_map/jit(_where)/select_n | solution.py:548
  42.4 7.1 %broadcast_select_fusion.1 = (bf16[768,3072]{1,0:T(8,128)(2,1)}, bf16[768,3072]{1,0:T(8,128)(2,1)}) fusion(bf16[768,3072]{1,0:T(8,128)(2,1)} %get-tuple-element.59, pred[]{:T(512)S(6)} %eq.21, bf16[1,768,3072]{2,1,0:T(8,128)(2,1)S(1)} %bitcast.69, pred[]{:T(512)S(6)} %eq.16), kind=kLoop, calls=%fused_computation.1 | loop fusion | flops 4718592 | bytes 18874370 | tf_op jit(solution)/shard_map/jit(_where)/select_n | solution.py:548
  49.5 6.6 %broadcast_select_fusion.4 = (bf16[768,2304]{1,0:T(8,128)(2,1)}, bf16[768,2304]{1,0:T(8,128)(2,1)}) fusion(bf16[768,2304]{1,0:T(8,128)(2,1)} %get-tuple-element.57, pred[]{:T(512)S(6)} %eq.21, bf16[1,768,2304]{2,1,0:T(8,128)(2,1)} %param.22, pred[]{:T(512)S(6)} %eq.16), kind=kLoop, calls=%fused_computation.4 | loop fusion | flops 3538944 | bytes 14155778 | tf_op jit(solution)/shard_map/jit(_where)/select_n | solution.py:548
  56.2 1.6 broadcast_select_fusion.6
  57.7 1.0 dynamic-slice_bitcast_fusion.1.x_ref
  58.8 1.0 dynamic-slice_bitcast_fusion.g_ref
  59.8 0.1 pad.57.clone
  59.9 1.0 maximum_maximum_fusion.cols_ref
  60.9 42.3 %fwd_layer.2 = (bf16[640,768]{1,0:T(8,128)(2,1)}, bf16[640,2304]{1,0:T(8,128)(2,1)}, f32[6,640,2]{2,1,0:T(8,128)}, bf16[640,768]{1,0:T(8,128)(2,1)}, f32[640,768...) custom-call(bf16[640,768]{1,0:T(8,128)(2,1)} %dynamic-slice_bitcast_fusion.1.x_ref, ...), custom_call_target="tpu_custom_call" | custom-call | tf_op jit(solution)/shard_map/fwd_layer/pallas_call | solution.py:164
  103.2 42.2 %fwd_layer.3 = (bf16[640,768]{1,0:T(8,128)(2,1)}, bf16[640,2304]{1,0:T(8,128)(2,1)}, f32[6,640,2]{2,1,0:T(8,128)}, bf16[640,768]{1,0:T(8,128)(2,1)}, f32[640,768...) custom-call(bf16[640,768]{1,0:T(8,128)(2,1)} %get-tuple-element.61.x_ref, ...), custom_call_target="tpu_custom_call" | custom-call | tf_op jit(solution)/shard_map/fwd_layer/pallas_call | solution.py:164
  145.4 37.1 %mlp_back.2 = (f32[640,768]{1,0:T(8,128)}, bf16[2,16,48,1536]{3,2,1,0:T(8,128)(2,1)}, bf16[2,3072,384]{2,1,0:T(8,128)(2,1)}, f32[8,3072]{1,0:T(8,128)}) custom-call(bf16[640,768]{1,0:T(8,128)(2,1)} %dynamic-slice_bitcast_fusion.g_ref, f32[640,128]{1,0:T(8,128)} %maximum_maximum_fusion.cols_ref, f32[8,3072]{1,0:T(8,128)} %get-tuple-element.128.par_ref, ...), custom_call_target="tpu_custom_call" | custom-call | tf_op jit(solution)/shard_map/mlp_back/pallas_call | solution.py:226
  182.5 37.6 %attn_back.2 = (bf16[640,768]{1,0:T(8,128)(2,1)}, bf16[2,16,48,1152]{3,2,1,0:T(8,128)(2,1)}, bf16[2,16,48,384]{3,2,1,0:T(8,128)(2,1)}, f32[8,3072]{1,0:T(8,128)}) custom-call(f32[640,768]{1,0:T(8,128)} %get-tuple-element.66.gmid_ref, f32[640,128]{1,0:T(8,128)} %maximum_maximum_fusion.cols_ref, f32[8,3072]{1,0:T(8,128)} %get-tuple-element.128.par_ref, ...), custom_call_target="tpu_custom_call" | custom-call | tf_op jit(solution)/shard_map/attn_back/pallas_call | solution.py:334
  220.1 36.9 %mlp_back.3 = (f32[640,768]{1,0:T(8,128)}, bf16[2,16,48,1536]{3,2,1,0:T(8,128)(2,1)}, bf16[2,3072,384]{2,1,0:T(8,128)(2,1)}, f32[8,3072]{1,0:T(8,128)}) custom-call(bf16[640,768]{1,0:T(8,128)(2,1)} %get-tuple-element.70.g_ref, f32[640,128]{1,0:T(8,128)} %maximum_maximum_fusion.cols_ref, f32[8,3072]{1,0:T(8,128)} %get-tuple-element.129.par_ref, ...), custom_call_target="tpu_custom_call" | custom-call | tf_op jit(solution)/shard_map/mlp_back/pallas_call | solution.py:226
  256.9 37.8 %attn_back.3 = (bf16[640,768]{1,0:T(8,128)(2,1)}, bf16[2,16,48,1152]{3,2,1,0:T(8,128)(2,1)}, bf16[2,16,48,384]{3,2,1,0:T(8,128)(2,1)}, f32[8,3072]{1,0:T(8,128)}) custom-call(f32[640,768]{1,0:T(8,128)} %get-tuple-element.74.gmid_ref, f32[640,128]{1,0:T(8,128)} %maximum_maximum_fusion.cols_ref, f32[8,3072]{1,0:T(8,128)} %get-tuple-element.129.par_ref, ...), custom_call_target="tpu_custom_call" | custom-call | tf_op jit(solution)/shard_map/attn_back/pallas_call | solution.py:334
  294.7 2.4 select_bitcast_fusion
  297.2 0.4 collective-permute-start.1
  297.5 1.5 select_bitcast_fusion.1
  299.0 0.1 collective-permute-start
  299.2 0.9 slice_reduce_fusion.13
  300.3 0.9 slice_reduce_fusion.10
  301.1 1.0 slice_reduce_fusion
  302.3 0.1 reshape_squeeze.43
  302.4 0.1 reshape_squeeze.44
  302.5 0.1 reshape_squeeze.45
  302.5 0.1 reshape_squeeze.46
  302.6 0.1 reshape_squeeze.48
  302.7 0.1 reshape_squeeze.54
  302.8 0.9 slice_reduce_fusion.5
  303.9 0.1 reshape_squeeze.50
  304.0 0.1 reshape_squeeze.51
  304.1 0.9 slice_reduce_fusion.2
  305.0 0.1 reshape_squeeze.52
  305.1 0.1 reshape_squeeze.55
  305.2 0.1 concatenate.61
  305.3 0.1 concatenate.65
  305.4 0.7 copy.39
  306.1 157.2 %reduce_grads.1 = (f32[48,2304]{1,0:T(8,128)}, f32[48,768]{1,0:T(8,128)}, f32[48,3072]{1,0:T(8,128)}, f32[192,768]{1,0:T(8,128)}, f32[8,128]{1,0:T(8,128)}) custom-call(bf16[2,4,2,2,192,384]{5,4,3,2,1,0:T(8,128)(2,1)} %bitcast.72, bf16[2,4,2,2,48,1536]{5,4,3,2,1,0:T(8,128)(2,1)} %bitcast.71, bf16[2,4,2,2,48,1152]{5,4,3,2,1,0:T(8,128)(2,1)} %bitcast.76, ...), custom_call_target="tpu_custom_call" | custom-call | tf_op jit(solution)/shard_map/reduce_grads/pallas_call | solution.py:520
  463.3 1.4 slice.110
  464.7 1.3 slice_bitcast_fusion.4
  466.0 1.5 slice_bitcast_fusion
  467.4 1.6 maximum_select_fusion.1
  469.1 3.3 maximum_select_fusion
  472.3 0.8 copy.44
  473.1 0.7 copy.45
  473.8 0.8 copy.46
  474.6 0.8 copy.47
  (62 shorter events, 0.8 us)
Async XLA Ops:
  0.6 57.1 %copy-start = (bf16[2,640,768]{2,1,0:T(8,128)(2,1)S(1)}, bf16[2,640,768]{2,1,0:T(8,128)(2,1)}, u32[]{:S(2)}) copy-start(bf16[2,640,768]{2,1,0:T(8,128)(2,1)} %param.16) | copy-start | bytes 5898244
  8.6 22.8 %copy-start.14 = (s32[2,640]{1,0:T(2,128)S(1)}, s32[2,640]{1,0:T(2,128)}, u32[]{:S(2)}) copy-start(s32[2,640]{1,0:T(2,128)} %param.17) | copy-start | bytes 15364
  8.6 24.0 %copy-start.8 = (f32[8,3072]{1,0:T(8,128)S(1)}, f32[8,3072]{1,0:T(8,128)}, u32[]{:S(2)}) copy-start(f32[8,3072]{1,0:T(8,128)} %stack.69.refs_4_) | copy-start | bytes 294916
  32.6 9.8 %slice-start = ((s8[4718592]{0:T(1024)(128)(4,1)}), s8[4194304]{0:T(1024)(128)(4,1)S(1)}, s32[]{:S(2)}) async-start(s8[4718592]{0:T(1024)(128)(4,1)} %bitcast.68), calls=%async_computation | async-start | bytes 8388608
  34.4 8.1 %slice-start.1 = ((s8[4718592]{0:T(1024)(128)(4,1)}), s8[524288]{0:T(1024)(128)(4,1)S(1)}, s32[]{:S(2)}) async-start(s8[4718592]{0:T(1024)(128)(4,1)} %bitcast.68), calls=%async_computation.1 | async-start | bytes 1048576
  49.5 6.6 %copy-start.3 = (bf16[1,768,768]{2,1,0:T(8,128)(2,1)S(1)}, bf16[1,768,768]{2,1,0:T(8,128)(2,1)}, u32[]{:S(2)}) copy-start(bf16[1,768,768]{2,1,0:T(8,128)(2,1)} %param.24) | copy-start | bytes 3538948
  49.5 6.6 %copy-start.6 = (bf16[768,768]{1,0:T(8,128)(2,1)S(1)}, bf16[768,768]{1,0:T(8,128)(2,1)}, u32[]{:S(2)}) copy-start(bf16[768,768]{1,0:T(8,128)(2,1)} %get-tuple-element.58) | copy-start | bytes 3538948
  56.2 2.6 copy-start.11
  256.9 37.8 %copy-start.4 = (bf16[640,768]{1,0:T(8,128)(2,1)S(1)}, bf16[640,768]{1,0:T(8,128)(2,1)}, u32[]{:S(2)}) copy-start(bf16[640,768]{1,0:T(8,128)(2,1)} %get-tuple-element.70.g_ref) | copy-start | bytes 2949124
  294.7 2.8 copy-start.2
  294.7 2.8 copy-start.7
  297.2 170.3 %collective-permute-start.1 = (bf16[640,768]{1,0:T(8,128)(2,1)}, bf16[640,768]{1,0:T(8,128)(2,1)S(1)}, u32[]{:S(2)}, u32[]{:S(2)}) collective-permute-start(bf16[640,768]{1,0:T(8,128)(2,1)} %get-tuple-element.125), channel_id=1, source_target_pairs={{0,16},{16,0},{1,17},{17,1},{2,18},{18,2},{3,19},{19,3},{4,20},{20... | collective-permute-start | bytes 2949128 | tf_op jit(solution)/shard_map/ppermute | solution.py:576
  299.0 170.0 %collective-permute-start = (bf16[640,768]{1,0:T(8,128)(2,1)}, bf16[640,768]{1,0:T(8,128)(2,1)}, u32[]{:S(2)}, u32[]{:S(2)}) collective-permute-start(bf16[640,768]{1,0:T(8,128)(2,1)} %get-tuple-element.127), channel_id=1, source_target_pairs={{0,16},{16,0},{1,17},{17,1},{2,18},{18,2},{3,19},{19,3},{4,20},{20... | collective-permute-start | bytes 2949128 | tf_op jit(solution)/shard_map/ppermute | solution.py:576
  463.3 5.7 %copy-start.5 = (bf16[1,1,640,768]{3,2,1,0:T(8,128)(2,1)S(1)}, bf16[1,1,640,768]{3,2,1,0:T(8,128)(2,1)}, u32[]{:S(2)}) copy-start(bf16[1,1,640,768]{3,2,1,0:T(8,128)(2,1)} %get-tuple-element.126) | copy-start | bytes 2949124
  469.0 3.3 copy-start.12
  469.0 4.1 copy-start.13
  469.0 4.7 copy-start.10
  469.0 5.5 %copy-start.9 = (f32[192,768]{1,0:T(8,128)S(1)}, f32[192,768]{1,0:T(8,128)}, u32[]{:S(2)}) copy-start(f32[192,768]{1,0:T(8,128)} %get-tuple-element.95) | copy-start | bytes 1769476
  469.1 6.3 %copy-start.1 = (bf16[2,640,768]{2,1,0:T(8,128)(2,1)S(1)}, bf16[2,640,768]{2,1,0:T(8,128)(2,1)}, u32[]{:S(2)}) copy-start(bf16[2,640,768]{2,1,0:T(8,128)(2,1)} %param.16) | copy-start | bytes 5898244
